TPU v7x, 256 devices: a whole 4x4x8 slice. The times are simulated.
256 devices in a mesh: outer: 4 (over z_hi), inner: 16 (over z_lo, x, core), head: 4 (over y).
Axes of the slice: x: 4, y: 4, z: 8 (z_hi: 4, z_lo: 2; z = z_hi * 2 + z_lo), core: 2. Of those that a mesh axis runs over, the one named last changes fastest.
Arguments:
- queries: bfloat16 [65536, 1024], P(('outer', 'inner'), 'head'), may hold values from -10 to 10
- keys: bfloat16 [65536, 128], P(('outer', 'inner', 'head')), may hold values from -10 to 10
- values: bfloat16 [65536, 128], P(('outer', 'inner', 'head')), may hold values from -6 to 6
- doc_lengths: int32 [28], replicated, may hold values from 1 to 3584, as said below
- block_count: int32 [64], replicated, may hold values from 1 to 2, as said below
Outputs:
- attended: bfloat16 [65536, 1024], P(('outer', 'inner'), 'head')
Inputs may be any that keep to these rules, and one draw needn't show every extreme that they name: `doc_lengths`: the lengths sum to 49152, and one rollout has exactly 3584 tokens. `block_count`: exactly half of the 64 context devices hold 2 blocks and the others 1; where 64 >= 16, 8 consecutive context devices hold 1 block each; the blocks follow one another in device order.
All inputs are finite; a program needn't handle non-finite values.
Results may differ from a plain program's by a relative error of at most 0.0032.
Values may be sent and summed in bfloat16 or wider, within the bound.
A program may use at most 64 MiB of HBM per device.

v0:
```python
import math

import jax
import jax.numpy as jnp
from jax import lax
from jax.sharding import PartitionSpec as P

BLOCK = 512
SLOTS = 2
REACH = 7


NEGATIVE = -1e30


def from_behind(value, axis, by):
    devices = lax.axis_size(axis)
    pairs = [(i, i + by) for i in range(devices) if 0 <= i + by < devices]
    return lax.ppermute(value, axis, pairs)


def located(block_count, source, count_rows):
    starts = jnp.cumsum(block_count) - block_count
    inside = source >= 0
    clipped = jnp.clip(source, 0, block_count.shape[0] - 1)
    offsets = jnp.arange(count_rows, dtype=jnp.int32)
    position = starts[clipped] * BLOCK + offsets
    is_live = inside & (offsets < block_count[clipped] * BLOCK)
    return (position, is_live)


def document(position, bounds):
    return jnp.sum((position[:, None] >= bounds[None, :]).astype(jnp.int32), axis=1)


def shards(queries, keys, values, doc_lengths, block_count):
    count_rows = queries.shape[0]
    head_dim = keys.shape[1]
    head_count = queries.shape[1] // head_dim
    block_rows = count_rows // SLOTS
    device = lax.axis_index(("outer", "inner"))
    bounds = jnp.cumsum(doc_lengths)
    own_pos, own_live = located(block_count, device, count_rows)
    own_doc = document(own_pos, bounds)
    full_keys, full_values = (
        lax.all_gather(keys, "head", axis=0, tiled=True),
        lax.all_gather(values, "head", axis=0, tiled=True),
    )
    own_unit = jnp.stack([full_keys, full_values])

    def relay_step(moving, unused):
        moving = from_behind(moving, ("outer", "inner"), 1)
        return (moving, moving)

    unused_last, earlier = lax.scan(relay_step, own_unit, None, length=REACH)
    window = jnp.concatenate([own_unit[None], earlier], axis=0)
    score_scale = 1.0 / math.sqrt(head_dim)
    query_rows = queries.reshape(count_rows, head_count, head_dim)

    def attend_block(running, key_block, value_block, key_pos, key_live, key_doc):
        visible = (
            own_live[:, None]
            & key_live[None, :]
            & (own_doc[:, None] == key_doc[None, :])
            & (key_pos[None, :] <= own_pos[:, None])
        )
        row_top, row_total, weighted = running
        scores = (
            jnp.einsum("qhd,kd->qhk", query_rows, key_block, preferred_element_type=jnp.float32)
            * score_scale
        )
        masked = jnp.where(visible[:, None, :], scores, NEGATIVE)
        new_top = jnp.maximum(row_top, jnp.max(masked, axis=2))
        factor = jnp.exp(row_top - new_top)
        weights = jnp.where(visible[:, None, :], jnp.exp(masked - new_top[:, :, None]), 0.0)
        row_total = row_total * factor + jnp.sum(weights, axis=2)
        weighted = weighted * factor[:, :, None] + jnp.einsum(
            "qhk,kd->qhd",
            weights.astype(jnp.bfloat16),
            value_block,
            preferred_element_type=jnp.float32,
        )
        return (new_top, row_total, weighted)

    def visit_unit(running, scan_entry):
        kv_piece, distance = scan_entry
        key_pos, key_live = located(block_count, device - distance, count_rows)
        key_doc = document(key_pos, bounds)
        for slot_index in range(SLOTS):
            row_start = slot_index * block_rows
            row_stop = row_start + block_rows
            running = attend_block(
                running,
                kv_piece[0, row_start:row_stop],
                kv_piece[1, row_start:row_stop],
                key_pos[row_start:row_stop],
                key_live[row_start:row_stop],
                key_doc[row_start:row_stop],
            )
        return (running, None)

    start_state = (
        jnp.full((count_rows, head_count), NEGATIVE, jnp.float32),
        jnp.zeros((count_rows, head_count), jnp.float32),
        jnp.zeros((count_rows, head_count, head_dim), jnp.float32),
    )
    finished, unused_out = lax.scan(
        visit_unit, start_state, (window, jnp.arange(REACH + 1, dtype=jnp.int32))
    )
    row_top, row_total, weighted = finished
    result = jnp.where(
        own_live[:, None, None],
        weighted / jnp.where(own_live[:, None], row_total, 1.0)[:, :, None],
        0.0,
    )
    return result.reshape(count_rows, head_count * head_dim).astype(jnp.bfloat16)


def solution(mesh):
    placed = (
        P(("outer", "inner"), "head"),
        P(("outer", "inner", "head"), None),
        P(("outer", "inner", "head"), None),
        P(),
        P(),
    )
    return jax.shard_map(
        shards, mesh=mesh, in_specs=placed, out_specs=P(("outer", "inner"), "head"), check_vma=False
    )
```

profile of v0, /device:TPU:128, one launch (start us, length us, event | category | flops | bytes accessed | tf_op | source)
XLA Modules:
  0.0 313.1 jit_solution(18314075608565028499)
XLA Ops:
  5.8 13.0 %all_gather.6 = bf16[1024,128]{1,0:T(8,128)(2,1)S(1)} all-gather(bf16[256,128]{1,0:T(8,128)(2,1)} %param.10), channel_id=1, replica_groups=mesh['outer'=4,'inner'=16,'head'=4] {'head'}, dimensions={0}, use_global_device_ids=true | all-gather | bytes 327680 | tf_op jit(solution)/shard_map/all_gather | solution.py:46
  18.8 12.5 %all_gather.7 = bf16[1024,128]{1,0:T(8,128)(2,1)S(1)} all-gather(bf16[256,128]{1,0:T(8,128)(2,1)} %param.11), channel_id=1, replica_groups=mesh['outer'=4,'inner'=16,'head'=4] {'head'}, dimensions={0}, use_global_device_ids=true | all-gather | bytes 327680 | tf_op jit(solution)/shard_map/all_gather | solution.py:47
  31.3 102.9 %while.29 = (s32[]{:T(128)}, bf16[2,1024,128]{2,1,0:T(8,128)(2,1)S(1)}, bf16[7,2,1024,128]{3,2,1,0:T(8,128)(2,1)}, s32[]{:T(128)}) while((s32[]{:T(128)}, bf16[2,1024,128]{2,1,0:T(8,128)(2,1)S(1)}, bf16[7,2,1024,128]{3,2,1,0:T(8,128)(2,1)}, s32[]{:T(128)}) %tuple.73), condition=%wide.region_1.2_spmd, body=%wide.region_0.0_spmd.sunk | while | flops 2 | bytes 4194409 | solution.py:55
  33.3 11.9 %collective-permute-done = bf16[2,1024,128]{2,1,0:T(8,128)(2,1)S(1)} collective-permute-done((bf16[2,1024,128]{2,1,0:T(8,128)(2,1)S(1)}, bf16[2,1024,128]{2,1,0:T(8,128)(2,1)S(1)}, u32[]{:S(2)}, u32[]{:S(2)}) %collective-permute-start) | collective-permute-done | bytes 524320 | tf_op jit(solution)/shard_map/while/body/eval_jaxpr/ppermute | solution.py:19
  47.9 11.9 %collective-permute-done = bf16[2,1024,128]{2,1,0:T(8,128)(2,1)S(1)} collective-permute-done((bf16[2,1024,128]{2,1,0:T(8,128)(2,1)S(1)}, bf16[2,1024,128]{2,1,0:T(8,128)(2,1)S(1)}, u32[]{:S(2)}, u32[]{:S(2)}) %collective-permute-start) | collective-permute-done | bytes 524320 | tf_op jit(solution)/shard_map/while/body/eval_jaxpr/ppermute | solution.py:19
  62.6 11.9 %collective-permute-done = bf16[2,1024,128]{2,1,0:T(8,128)(2,1)S(1)} collective-permute-done((bf16[2,1024,128]{2,1,0:T(8,128)(2,1)S(1)}, bf16[2,1024,128]{2,1,0:T(8,128)(2,1)S(1)}, u32[]{:S(2)}, u32[]{:S(2)}) %collective-permute-start) | collective-permute-done | bytes 524320 | tf_op jit(solution)/shard_map/while/body/eval_jaxpr/ppermute | solution.py:19
  77.3 11.9 %collective-permute-done = bf16[2,1024,128]{2,1,0:T(8,128)(2,1)S(1)} collective-permute-done((bf16[2,1024,128]{2,1,0:T(8,128)(2,1)S(1)}, bf16[2,1024,128]{2,1,0:T(8,128)(2,1)S(1)}, u32[]{:S(2)}, u32[]{:S(2)}) %collective-permute-start) | collective-permute-done | bytes 524320 | tf_op jit(solution)/shard_map/while/body/eval_jaxpr/ppermute | solution.py:19
  92.0 11.9 %collective-permute-done = bf16[2,1024,128]{2,1,0:T(8,128)(2,1)S(1)} collective-permute-done((bf16[2,1024,128]{2,1,0:T(8,128)(2,1)S(1)}, bf16[2,1024,128]{2,1,0:T(8,128)(2,1)S(1)}, u32[]{:S(2)}, u32[]{:S(2)}) %collective-permute-start) | collective-permute-done | bytes 524320 | tf_op jit(solution)/shard_map/while/body/eval_jaxpr/ppermute | solution.py:19
  106.7 11.9 %collective-permute-done = bf16[2,1024,128]{2,1,0:T(8,128)(2,1)S(1)} collective-permute-done((bf16[2,1024,128]{2,1,0:T(8,128)(2,1)S(1)}, bf16[2,1024,128]{2,1,0:T(8,128)(2,1)S(1)}, u32[]{:S(2)}, u32[]{:S(2)}) %collective-permute-start) | collective-permute-done | bytes 524320 | tf_op jit(solution)/shard_map/while/body/eval_jaxpr/ppermute | solution.py:19
  121.4 11.9 %collective-permute-done = bf16[2,1024,128]{2,1,0:T(8,128)(2,1)S(1)} collective-permute-done((bf16[2,1024,128]{2,1,0:T(8,128)(2,1)S(1)}, bf16[2,1024,128]{2,1,0:T(8,128)(2,1)S(1)}, u32[]{:S(2)}, u32[]{:S(2)}) %collective-permute-start) | collective-permute-done | bytes 524320 | tf_op jit(solution)/shard_map/while/body/eval_jaxpr/ppermute | solution.py:19
  134.2 4.4 %pad_maximum_fusion = bf16[8,2,1024,128]{3,2,1,0:T(8,128)(2,1)} fusion(bf16[7,2,1024,128]{3,2,1,0:T(8,128)(2,1)} %get-tuple-element.177, bf16[1,2,1024,128]{3,2,1,0:T(8,128)(2,1)S(1)} %get-tuple-element.320), kind=kLoop, calls=%fused_computation.51 | loop fusion | flops 2097152 | bytes 8388608 | tf_op jit(solution)/shard_map/concatenate | solution.py:56
  139.1 172.4 %while.30 = (s32[]{:T(128)}, f32[1024,2]{0,1:T(2,128)S(1)}, f32[1024,2]{0,1:T(2,128)S(1)}, f32[1024,2,128]{2,0,1:T(8,128)S(1)}, s32[8]{0:T(128)S(1)}, /*index=5*...) while((s32[]{:T(128)}, f32[1024,2]{0,1:T(2,128)S(1)}, ...), condition=%wide.region_11.12_spmd.clone, body=%wide.region_5.11_spmd.clone.sunk | while | flops 1107663872 | bytes 69999072 | solution.py:107
  151.5 3.8 %fusion.80 = f32[1024,2,128]{2,0,1:T(8,128)S(1)} fusion(f32[512,1024,2]{1,0,2:T(8,128)} %get-tuple-element.464, f32[1024,2]{0,1:T(2,128)S(1)} %get-tuple-element.521, pred[1024,512]{0,1:T(8,128)(4,1)S(1)} %get-tuple-element.457, bf16[2,1024,128]{2,1,0:T(8,128)(2,1)S(1)} %dynamic-slice_bitcast_fusion.2), kind=kOutput, calls=%fused_computation.13.clone.1 | convolution fusion | flops 273678336 | bytes 5906432 | tf_op jit(solution)/shard_map/while/body/eval_jaxpr/qhk,kd->qhd/dot_general | solution.py:77
  170.1 2.9 fusion.76
  173.0 3.8 %fusion.80 = f32[1024,2,128]{2,0,1:T(8,128)S(1)} fusion(f32[512,1024,2]{1,0,2:T(8,128)} %get-tuple-element.464, f32[1024,2]{0,1:T(2,128)S(1)} %get-tuple-element.521, pred[1024,512]{0,1:T(8,128)(4,1)S(1)} %get-tuple-element.457, bf16[2,1024,128]{2,1,0:T(8,128)(2,1)S(1)} %dynamic-slice_bitcast_fusion.2), kind=kOutput, calls=%fused_computation.13.clone.1 | convolution fusion | flops 273678336 | bytes 5906432 | tf_op jit(solution)/shard_map/while/body/eval_jaxpr/qhk,kd->qhd/dot_general | solution.py:77
  194.6 3.8 %fusion.80 = f32[1024,2,128]{2,0,1:T(8,128)S(1)} fusion(f32[512,1024,2]{1,0,2:T(8,128)} %get-tuple-element.464, f32[1024,2]{0,1:T(2,128)S(1)} %get-tuple-element.521, pred[1024,512]{0,1:T(8,128)(4,1)S(1)} %get-tuple-element.457, bf16[2,1024,128]{2,1,0:T(8,128)(2,1)S(1)} %dynamic-slice_bitcast_fusion.2), kind=kOutput, calls=%fused_computation.13.clone.1 | convolution fusion | flops 273678336 | bytes 5906432 | tf_op jit(solution)/shard_map/while/body/eval_jaxpr/qhk,kd->qhd/dot_general | solution.py:77
  213.2 2.9 fusion.76
  216.1 3.8 %fusion.80 = f32[1024,2,128]{2,0,1:T(8,128)S(1)} fusion(f32[512,1024,2]{1,0,2:T(8,128)} %get-tuple-element.464, f32[1024,2]{0,1:T(2,128)S(1)} %get-tuple-element.521, pred[1024,512]{0,1:T(8,128)(4,1)S(1)} %get-tuple-element.457, bf16[2,1024,128]{2,1,0:T(8,128)(2,1)S(1)} %dynamic-slice_bitcast_fusion.2), kind=kOutput, calls=%fused_computation.13.clone.1 | convolution fusion | flops 273678336 | bytes 5906432 | tf_op jit(solution)/shard_map/while/body/eval_jaxpr/qhk,kd->qhd/dot_general | solution.py:77
  237.7 3.8 %fusion.80 = f32[1024,2,128]{2,0,1:T(8,128)S(1)} fusion(f32[512,1024,2]{1,0,2:T(8,128)} %get-tuple-element.464, f32[1024,2]{0,1:T(2,128)S(1)} %get-tuple-element.521, pred[1024,512]{0,1:T(8,128)(4,1)S(1)} %get-tuple-element.457, bf16[2,1024,128]{2,1,0:T(8,128)(2,1)S(1)} %dynamic-slice_bitcast_fusion.2), kind=kOutput, calls=%fused_computation.13.clone.1 | convolution fusion | flops 273678336 | bytes 5906432 | tf_op jit(solution)/shard_map/while/body/eval_jaxpr/qhk,kd->qhd/dot_general | solution.py:77
  256.3 2.9 fusion.76
  259.3 3.8 %fusion.80 = f32[1024,2,128]{2,0,1:T(8,128)S(1)} fusion(f32[512,1024,2]{1,0,2:T(8,128)} %get-tuple-element.464, f32[1024,2]{0,1:T(2,128)S(1)} %get-tuple-element.521, pred[1024,512]{0,1:T(8,128)(4,1)S(1)} %get-tuple-element.457, bf16[2,1024,128]{2,1,0:T(8,128)(2,1)S(1)} %dynamic-slice_bitcast_fusion.2), kind=kOutput, calls=%fused_computation.13.clone.1 | convolution fusion | flops 273678336 | bytes 5906432 | tf_op jit(solution)/shard_map/while/body/eval_jaxpr/qhk,kd->qhd/dot_general | solution.py:77
  280.8 3.8 %fusion.80 = f32[1024,2,128]{2,0,1:T(8,128)S(1)} fusion(f32[512,1024,2]{1,0,2:T(8,128)} %get-tuple-element.464, f32[1024,2]{0,1:T(2,128)S(1)} %get-tuple-element.521, pred[1024,512]{0,1:T(8,128)(4,1)S(1)} %get-tuple-element.457, bf16[2,1024,128]{2,1,0:T(8,128)(2,1)S(1)} %dynamic-slice_bitcast_fusion.2), kind=kOutput, calls=%fused_computation.13.clone.1 | convolution fusion | flops 273678336 | bytes 5906432 | tf_op jit(solution)/shard_map/while/body/eval_jaxpr/qhk,kd->qhd/dot_general | solution.py:77
  299.4 2.9 fusion.76
  302.4 3.8 %fusion.80 = f32[1024,2,128]{2,0,1:T(8,128)S(1)} fusion(f32[512,1024,2]{1,0,2:T(8,128)} %get-tuple-element.464, f32[1024,2]{0,1:T(2,128)S(1)} %get-tuple-element.521, pred[1024,512]{0,1:T(8,128)(4,1)S(1)} %get-tuple-element.457, bf16[2,1024,128]{2,1,0:T(8,128)(2,1)S(1)} %dynamic-slice_bitcast_fusion.2), kind=kOutput, calls=%fused_computation.13.clone.1 | convolution fusion | flops 273678336 | bytes 5906432 | tf_op jit(solution)/shard_map/while/body/eval_jaxpr/qhk,kd->qhd/dot_general | solution.py:77
  (235 shorter events, 140.1 us)
Async XLA Ops:
  31.3 13.8 %collective-permute-start = (bf16[2,1024,128]{2,1,0:T(8,128)(2,1)S(1)}, bf16[2,1024,128]{2,1,0:T(8,128)(2,1)S(1)}, u32[]{:S(2)}, u32[]{:S(2)}) collective-permute-start(bf16[2,1024,128]{2,1,0:T(8,128)(2,1)S(1)} %get-tuple-element.475), channel_id=1, source_target_pairs={{0,4},{4,8},{8,12},{12,16},{16,20},{20,24},{24,28},{28,32},{32,36}... | collective-permute-start | bytes 1572872 | tf_op jit(solution)/shard_map/while/body/eval_jaxpr/ppermute | solution.py:19
  46.0 13.8 %collective-permute-start = (bf16[2,1024,128]{2,1,0:T(8,128)(2,1)S(1)}, bf16[2,1024,128]{2,1,0:T(8,128)(2,1)S(1)}, u32[]{:S(2)}, u32[]{:S(2)}) collective-permute-start(bf16[2,1024,128]{2,1,0:T(8,128)(2,1)S(1)} %get-tuple-element.475), channel_id=1, source_target_pairs={{0,4},{4,8},{8,12},{12,16},{16,20},{20,24},{24,28},{28,32},{32,36}... | collective-permute-start | bytes 1572872 | tf_op jit(solution)/shard_map/while/body/eval_jaxpr/ppermute | solution.py:19
  60.7 13.8 %collective-permute-start = (bf16[2,1024,128]{2,1,0:T(8,128)(2,1)S(1)}, bf16[2,1024,128]{2,1,0:T(8,128)(2,1)S(1)}, u32[]{:S(2)}, u32[]{:S(2)}) collective-permute-start(bf16[2,1024,128]{2,1,0:T(8,128)(2,1)S(1)} %get-tuple-element.475), channel_id=1, source_target_pairs={{0,4},{4,8},{8,12},{12,16},{16,20},{20,24},{24,28},{28,32},{32,36}... | collective-permute-start | bytes 1572872 | tf_op jit(solution)/shard_map/while/body/eval_jaxpr/ppermute | solution.py:19
  75.4 13.8 %collective-permute-start = (bf16[2,1024,128]{2,1,0:T(8,128)(2,1)S(1)}, bf16[2,1024,128]{2,1,0:T(8,128)(2,1)S(1)}, u32[]{:S(2)}, u32[]{:S(2)}) collective-permute-start(bf16[2,1024,128]{2,1,0:T(8,128)(2,1)S(1)} %get-tuple-element.475), channel_id=1, source_target_pairs={{0,4},{4,8},{8,12},{12,16},{16,20},{20,24},{24,28},{28,32},{32,36}... | collective-permute-start | bytes 1572872 | tf_op jit(solution)/shard_map/while/body/eval_jaxpr/ppermute | solution.py:19
  90.1 13.8 %collective-permute-start = (bf16[2,1024,128]{2,1,0:T(8,128)(2,1)S(1)}, bf16[2,1024,128]{2,1,0:T(8,128)(2,1)S(1)}, u32[]{:S(2)}, u32[]{:S(2)}) collective-permute-start(bf16[2,1024,128]{2,1,0:T(8,128)(2,1)S(1)} %get-tuple-element.475), channel_id=1, source_target_pairs={{0,4},{4,8},{8,12},{12,16},{16,20},{20,24},{24,28},{28,32},{32,36}... | collective-permute-start | bytes 1572872 | tf_op jit(solution)/shard_map/while/body/eval_jaxpr/ppermute | solution.py:19
  104.8 13.8 %collective-permute-start = (bf16[2,1024,128]{2,1,0:T(8,128)(2,1)S(1)}, bf16[2,1024,128]{2,1,0:T(8,128)(2,1)S(1)}, u32[]{:S(2)}, u32[]{:S(2)}) collective-permute-start(bf16[2,1024,128]{2,1,0:T(8,128)(2,1)S(1)} %get-tuple-element.475), channel_id=1, source_target_pairs={{0,4},{4,8},{8,12},{12,16},{16,20},{20,24},{24,28},{28,32},{32,36}... | collective-permute-start | bytes 1572872 | tf_op jit(solution)/shard_map/while/body/eval_jaxpr/ppermute | solution.py:19
  119.5 13.8 %collective-permute-start = (bf16[2,1024,128]{2,1,0:T(8,128)(2,1)S(1)}, bf16[2,1024,128]{2,1,0:T(8,128)(2,1)S(1)}, u32[]{:S(2)}, u32[]{:S(2)}) collective-permute-start(bf16[2,1024,128]{2,1,0:T(8,128)(2,1)S(1)} %get-tuple-element.475), channel_id=1, source_target_pairs={{0,4},{4,8},{8,12},{12,16},{16,20},{20,24},{24,28},{28,32},{32,36}... | collective-permute-start | bytes 1572872 | tf_op jit(solution)/shard_map/while/body/eval_jaxpr/ppermute | solution.py:19
  134.2 4.4 %copy-start.2 = (bf16[1024,256]{1,0:T(8,128)(2,1)S(1)}, bf16[1024,256]{1,0:T(8,128)(2,1)}, u32[]{:S(2)}) copy-start(bf16[1024,256]{1,0:T(8,128)(2,1)} %param.9) | copy-start | bytes 1572868
  134.2 4.9 %copy-start.3 = (s32[64]{0:T(128)S(1)}, s32[64]{0:T(128)}, u32[]{:S(2)}) copy-start(s32[64]{0:T(128)} %param.13) | copy-start | bytes 772
  151.5 4.7 %copy-start.1 = (f32[512,1024,2]{1,0,2:T(8,128)S(1)}, f32[512,1024,2]{1,0,2:T(8,128)}, u32[]{:S(2)}) copy-start(f32[512,1024,2]{1,0,2:T(8,128)} %get-tuple-element.464) | copy-start | bytes 12582916 | tf_op jit(solution)/shard_map/while
  173.0 3.9 %copy-start = (f32[512,1024,2]{1,0,2:T(8,128)S(1)}, f32[512,1024,2]{1,0,2:T(8,128)}, u32[]{:S(2)}) copy-start(f32[512,1024,2]{1,0,2:T(8,128)} %get-tuple-element.462) | copy-start | bytes 12582916 | tf_op jit(solution)/shard_map/while
  173.0 4.7 %copy-start.1 = (f32[512,1024,2]{1,0,2:T(8,128)S(1)}, f32[512,1024,2]{1,0,2:T(8,128)}, u32[]{:S(2)}) copy-start(f32[512,1024,2]{1,0,2:T(8,128)} %get-tuple-element.464) | copy-start | bytes 12582916 | tf_op jit(solution)/shard_map/while
  194.6 3.9 %copy-start = (f32[512,1024,2]{1,0,2:T(8,128)S(1)}, f32[512,1024,2]{1,0,2:T(8,128)}, u32[]{:S(2)}) copy-start(f32[512,1024,2]{1,0,2:T(8,128)} %get-tuple-element.462) | copy-start | bytes 12582916 | tf_op jit(solution)/shard_map/while
  194.6 4.7 %copy-start.1 = (f32[512,1024,2]{1,0,2:T(8,128)S(1)}, f32[512,1024,2]{1,0,2:T(8,128)}, u32[]{:S(2)}) copy-start(f32[512,1024,2]{1,0,2:T(8,128)} %get-tuple-element.464) | copy-start | bytes 12582916 | tf_op jit(solution)/shard_map/while
  216.1 3.9 %copy-start = (f32[512,1024,2]{1,0,2:T(8,128)S(1)}, f32[512,1024,2]{1,0,2:T(8,128)}, u32[]{:S(2)}) copy-start(f32[512,1024,2]{1,0,2:T(8,128)} %get-tuple-element.462) | copy-start | bytes 12582916 | tf_op jit(solution)/shard_map/while
  216.1 4.7 %copy-start.1 = (f32[512,1024,2]{1,0,2:T(8,128)S(1)}, f32[512,1024,2]{1,0,2:T(8,128)}, u32[]{:S(2)}) copy-start(f32[512,1024,2]{1,0,2:T(8,128)} %get-tuple-element.464) | copy-start | bytes 12582916 | tf_op jit(solution)/shard_map/while
  237.7 3.9 %copy-start = (f32[512,1024,2]{1,0,2:T(8,128)S(1)}, f32[512,1024,2]{1,0,2:T(8,128)}, u32[]{:S(2)}) copy-start(f32[512,1024,2]{1,0,2:T(8,128)} %get-tuple-element.462) | copy-start | bytes 12582916 | tf_op jit(solution)/shard_map/while
  237.7 4.7 %copy-start.1 = (f32[512,1024,2]{1,0,2:T(8,128)S(1)}, f32[512,1024,2]{1,0,2:T(8,128)}, u32[]{:S(2)}) copy-start(f32[512,1024,2]{1,0,2:T(8,128)} %get-tuple-element.464) | copy-start | bytes 12582916 | tf_op jit(solution)/shard_map/while
  259.2 3.9 %copy-start = (f32[512,1024,2]{1,0,2:T(8,128)S(1)}, f32[512,1024,2]{1,0,2:T(8,128)}, u32[]{:S(2)}) copy-start(f32[512,1024,2]{1,0,2:T(8,128)} %get-tuple-element.462) | copy-start | bytes 12582916 | tf_op jit(solution)/shard_map/while
  259.2 4.7 %copy-start.1 = (f32[512,1024,2]{1,0,2:T(8,128)S(1)}, f32[512,1024,2]{1,0,2:T(8,128)}, u32[]{:S(2)}) copy-start(f32[512,1024,2]{1,0,2:T(8,128)} %get-tuple-element.464) | copy-start | bytes 12582916 | tf_op jit(solution)/shard_map/while
  280.8 3.9 %copy-start = (f32[512,1024,2]{1,0,2:T(8,128)S(1)}, f32[512,1024,2]{1,0,2:T(8,128)}, u32[]{:S(2)}) copy-start(f32[512,1024,2]{1,0,2:T(8,128)} %get-tuple-element.462) | copy-start | bytes 12582916 | tf_op jit(solution)/shard_map/while
  280.8 4.7 %copy-start.1 = (f32[512,1024,2]{1,0,2:T(8,128)S(1)}, f32[512,1024,2]{1,0,2:T(8,128)}, u32[]{:S(2)}) copy-start(f32[512,1024,2]{1,0,2:T(8,128)} %get-tuple-element.464) | copy-start | bytes 12582916 | tf_op jit(solution)/shard_map/while
  302.3 3.9 %copy-start = (f32[512,1024,2]{1,0,2:T(8,128)S(1)}, f32[512,1024,2]{1,0,2:T(8,128)}, u32[]{:S(2)}) copy-start(f32[512,1024,2]{1,0,2:T(8,128)} %get-tuple-element.462) | copy-start | bytes 12582916 | tf_op jit(solution)/shard_map/while
  302.4 4.7 %copy-start.1 = (f32[512,1024,2]{1,0,2:T(8,128)S(1)}, f32[512,1024,2]{1,0,2:T(8,128)}, u32[]{:S(2)}) copy-start(f32[512,1024,2]{1,0,2:T(8,128)} %get-tuple-element.464) | copy-start | bytes 12582916 | tf_op jit(solution)/shard_map/while
  (1 other events, 3.9 us)
where the time goes:
time: 314 us; the launch traced here: 313 us
  matrix products  94.8 us (30%)
  waiting for transfers between devices  83.2 us (26%)
  local copies, waits for them, and re-layouts  40.1 us (13%)
  other arithmetic  38.6 us (12%)
  blocking collectives  25.4 us (8%)
  loops' own time  16.2 us (5%)
  starting transfers between devices  13.4 us (4%)
    ppermute x7, waiting for transfers between devices, from_behind(): return lax.ppermute(value, axis, pairs)  83.2 us
    dot_general x16, matrix products, attend_block(): jnp.einsum('qhk,kd->qhd', weights.astype(jnp.bfloat16), value_block, pref...  48 us
    dot_general x16, matrix products, attend_block(): jnp.einsum('qhd,kd->qhk', query_rows, key_block, preferred_element_type=j...  46.8 us
    reduce_sum x8, other arithmetic, attend_block(): row_total = row_total * factor + jnp.sum(weights, axis=2)  17.9 us
    another operation x1, loops' own time, shards(): lax.scan(visit_unit, start_state, (window, jnp.arange(REACH + 1, dtype=jn...  16.1 us
    ppermute x7, starting transfers between devices, from_behind(): return lax.ppermute(value, axis, pairs)  13.4 us
    all_gather x1, blocking collectives, shards(): lax.all_gather(keys, 'head', axis=0, tiled=True)  13 us
    all_gather x1, blocking collectives, shards(): lax.all_gather(values, 'head', axis=0, tiled=True)  12.5 us
  transfers between devices with their start and end apart: 7, of which 7 were waited for; matrix products, arithmetic and copies ran while one was open for 0% of the time, Pallas kernels for 0%

commit v1 on v0

v1 whole, which is shorter than its diff:
```python
import math

import jax
import jax.numpy as jnp
from jax import lax
from jax.experimental import pallas as pl
from jax.experimental.pallas import tpu as pltpu
from jax.sharding import PartitionSpec as P

BLOCK = 512
SLOTS = 2
REACH = 7
QUARTER = 256
HALF = 128
MESH = pl.DeviceIdType.MESH
NEGATIVE = -1e30


def gather_kernel(k_ref, v_ref, kw, vw, send_sems, recv_sems, local_sems):
    outer = lax.axis_index("outer")
    inner = lax.axis_index("inner")
    y = lax.axis_index("head")
    z = outer * 2 + inner // 8
    x = lax.rem(inner // 2, 4)
    core = lax.rem(inner, 2)

    def place(px, py, pz, pc):
        return (pz // 2, lax.rem(pz, 2) * 8 + px * 2 + pc, py)

    xp, xm = lax.rem(x + 1, 4), lax.rem(x + 3, 4)
    yp, ym = lax.rem(y + 1, 4), lax.rem(y + 3, 4)
    zp, zm = lax.rem(z + 1, 8), lax.rem(z + 7, 8)
    z_next = jnp.where(x == 3, zp, z)
    z_prev = jnp.where(x == 0, zm, z)
    right, left = place(xp, y, z, core), place(xm, y, z, core)
    up, down = place(x, y, zp, core), place(x, y, zm, core)
    after, before = place(x, yp, z, core), place(x, ym, z, core)
    follower, leader = place(xp, y, z_next, core), place(xm, y, z_prev, core)
    sibling = place(x, y, z, 1 - core)

    barrier = pltpu.get_barrier_semaphore()
    for partner in (right, left, up, down, after, before, follower, leader, sibling):
        pl.semaphore_signal(barrier, inc=1, device_id=partner, device_id_type=MESH)

    def rows(order, half=None):
        start = lax.rem(y + order, 4) * QUARTER
        if half is None:
            return pl.ds(pl.multiple_of(start, QUARTER), QUARTER)
        return pl.ds(pl.multiple_of(start + half * HALF, HALF), HALF)

    used = []

    def transfer(src, dst, device, sem=None):
        if sem is None:
            sem = len(used)
            used.append(sem)
        return pltpu.make_async_remote_copy(
            src_ref=src,
            dst_ref=dst,
            send_sem=send_sems.at[sem],
            recv_sem=recv_sems.at[sem],
            device_id=device,
            device_id_type=MESH,
        )

    sent = []

    def go(copy):
        copy.start()
        sent.append(copy)
        return copy

    keep_k = pltpu.make_async_copy(k_ref, kw.at[0, rows(0)], local_sems.at[0])
    keep_v = pltpu.make_async_copy(v_ref, vw.at[0, rows(0)], local_sems.at[1])
    keep_k.start()
    keep_v.start()
    pl.semaphore_wait(barrier, 9)

    def ring_open(src, win, slot):
        return (
            go(transfer(src, win.at[slot, rows(0)], after)),
            go(transfer(src, win.at[slot, rows(0)], before)),
        )

    def ring_pass(win, slot, opened):
        opened[0].wait_recv()
        first = go(transfer(win.at[slot, rows(3, 0)], win.at[slot, rows(3, 0)], after))
        opened[1].wait_recv()
        second = go(transfer(win.at[slot, rows(1, 1)], win.at[slot, rows(1, 1)], before))
        return first, second

    def ring_close(passed):
        passed[0].wait_recv()
        passed[1].wait_recv()

    def climb(src, win, part):
        return go(transfer(src, win.at[8, part], up))

    class Sideways:
        def __init__(self, win, part, own):
            raised = win.at[8, part]
            self.right = (
                transfer(own, win.at[2, part], right),
                transfer(raised, win.at[2, part], right, len(used) - 1),
            )
            self.left = (
                transfer(own, win.at[6, part], left),
                transfer(raised, win.at[6, part], left, len(used) - 1),
            )

        def from_own(self):
            pl.when(x < 3)(self.right[0].start)
            pl.when(x == 0)(self.left[0].start)
            sent.extend((self.right[0], self.left[0]))

        def from_raised(self):
            pl.when(x == 3)(self.right[1].start)
            pl.when(x > 0)(self.left[1].start)

    k_open = ring_open(k_ref, kw, 0)
    v_parts = (rows(0, 0), rows(0, 1))
    v_src = (v_ref.at[pl.ds(0, HALF)], v_ref.at[pl.ds(HALF, HALF)])
    v_up, v_side = [], []
    for src, part in zip(v_src, v_parts):
        v_up.append(climb(src, vw, part))
        v_side.append(Sideways(vw, part, src))
        v_side[-1].from_own()

    def share(win, slot, base):
        def start(index):
            copy = transfer(win.at[slot], win.at[2 * index + 1], sibling, base + index)
            copy.start()

        if slot == 0:
            pl.when(core == 0)(lambda: start(0))
        elif slot == 8:
            pl.when(core == 1)(lambda: start(3))
        else:
            start(slot // 2 - core)

    k_share, v_share = len(used), len(used) + 4
    used.extend(range(len(used), len(used) + 8))

    k_up, k_side = [], []

    def key_chunk(order, src):
        k_up.append(climb(src, kw, rows(order)))
        k_side.append(Sideways(kw, rows(order), src))
        k_side[-1].from_own()

    key_chunk(0, k_ref)
    v0 = ring_open(v_ref, vw, 0)
    keep_k.wait()
    keep_v.wait()

    k_open[0].wait_recv()
    k_pass0 = go(transfer(kw.at[0, rows(3, 0)], kw.at[0, rows(3, 0)], after))
    key_chunk(3, kw.at[0, rows(3)])
    k_open[1].wait_recv()
    k_pass1 = go(transfer(kw.at[0, rows(1, 1)], kw.at[0, rows(1, 1)], before))
    key_chunk(1, kw.at[0, rows(1)])

    for copy, side in zip(v_up, v_side):
        copy.wait_recv()
        side.from_raised()

    k_pass0.wait_recv()
    k_pass1.wait_recv()
    key_chunk(2, kw.at[0, rows(2)])
    share(kw, 0, k_share)

    v_side[0].right[0].wait_recv()
    v_mid0 = go(transfer(vw.at[2, v_parts[0]], vw.at[4, v_parts[0]], follower))
    v_side[1].right[0].wait_recv()
    v2 = ring_open(vw.at[2, rows(0)], vw, 2)
    v_side[1].left[0].wait_recv()
    v_mid1 = go(transfer(vw.at[6, v_parts[1]], vw.at[4, v_parts[1]], leader))
    v_side[0].left[0].wait_recv()

    k_up[0].wait_recv()
    k_side[0].from_raised()
    v0p = ring_pass(vw, 0, v0)
    v6 = ring_open(vw.at[6, rows(0)], vw, 6)
    k_up[1].wait_recv()
    k_side[1].from_raised()

    k_mid = [None] * 4
    orders = (0, 3, 1, 2)

    def relay_right(i):
        k_side[i].right[0].wait_recv()
        part = rows(orders[i])
        k_mid[i] = go(transfer(kw.at[2, part], kw.at[4, part], follower))

    def relay_left(i):
        k_side[i].left[0].wait_recv()
        part = rows(orders[i])
        k_mid[i] = go(transfer(kw.at[6, part], kw.at[4, part], leader))

    relay_right(0)
    v_mid0.wait_recv()
    v_mid1.wait_recv()
    v4 = ring_open(vw.at[4, rows(0)], vw, 4)
    v2p = ring_pass(vw, 2, v2)
    k_up[2].wait_recv()
    k_side[2].from_raised()
    ring_close(v0p)
    share(vw, 0, v_share)
    relay_right(1)
    k_up[3].wait_recv()
    k_side[3].from_raised()
    v6p = ring_pass(vw, 6, v6)

    far = len(used)
    used.extend(range(far, far + 4))
    far_open = (
        transfer(vw.at[8, rows(0)], vw.at[8, rows(0)], after, far),
        transfer(vw.at[8, rows(0)], vw.at[8, rows(0)], before, far + 1),
    )
    far_pass = (
        transfer(vw.at[8, rows(3, 0)], vw.at[8, rows(3, 0)], after, far + 2),
        transfer(vw.at[8, rows(1, 1)], vw.at[8, rows(1, 1)], before, far + 3),
    )

    @pl.when(core == 1)
    def _():
        far_open[0].start()
        far_open[1].start()

    ring_close(v2p)
    share(vw, 2, v_share)
    relay_left(2)
    share(kw, 8, k_share)
    v4p = ring_pass(vw, 4, v4)
    relay_left(3)
    k_side[2].right[0].wait_recv()
    k_side[3].right[0].wait_recv()
    share(kw, 2, k_share)

    @pl.when(core == 1)
    def _():
        far_open[0].wait_recv()
        far_pass[0].start()
        far_open[1].wait_recv()
        far_pass[1].start()

    ring_close(v6p)
    share(vw, 6, v_share)
    k_side[0].left[0].wait_recv()
    k_side[1].left[0].wait_recv()
    share(kw, 6, k_share)
    ring_close(v4p)
    share(vw, 4, v_share)

    @pl.when(core == 1)
    def _():
        far_pass[0].wait_recv()
        far_pass[1].wait_recv()

    share(vw, 8, v_share)
    for copy in k_mid:
        copy.wait_recv()
    share(kw, 4, k_share)

    for base, win in ((k_share, kw), (v_share, vw)):
        for index in range(4):
            copy = transfer(win.at[2 * index + 1], win.at[2 * index + 1], sibling, base + index)
            copy.wait_recv()
            copy.wait_send()
    for copy in sent:
        copy.wait_send()

    @pl.when(core == 1)
    def _():
        for copy in far_open + far_pass:
            copy.wait_send()


def gather_windows(keys, values):
    depth = keys.shape[1]
    window = jax.ShapeDtypeStruct((REACH + 2, BLOCK * SLOTS, depth), keys.dtype)
    count = 96
    return pl.pallas_call(
        gather_kernel,
        out_shape=(window, window),
        in_specs=[pl.BlockSpec(memory_space=pl.ANY)] * 2,
        out_specs=(pl.BlockSpec(memory_space=pl.ANY),) * 2,
        scratch_shapes=[
            pltpu.SemaphoreType.DMA((count,)),
            pltpu.SemaphoreType.DMA((count,)),
            pltpu.SemaphoreType.DMA((2,)),
        ],
        compiler_params=pltpu.CompilerParams(collective_id=0, has_side_effects=True),
        name="gather_windows",
    )(keys, values)


def attend_kernel(
    lengths, counts, q_ref, kw, vw, out_ref, kbuf, vbuf, scores, top, total, first, table, sems
):
    heads = q_ref.shape[1] // 128
    inner = lax.axis_index("inner")
    me = lax.axis_index("outer") * 16 + inner
    count = counts[me]
    before = lax.fori_loop(0, me, lambda i, t: t + counts[i], 0)
    base = before * BLOCK
    docs = lengths.shape[0]

    table[0] = 1
    table[1] = 0
    filled = jnp.int32(2)
    for distance in range(1, REACH + 1):
        source = me - distance
        held = jnp.where(source >= 0, counts[jnp.maximum(source, 0)], 0)
        table[filled] = distance * SLOTS + held - 1
        table[filled + 1] = distance * SLOTS
        filled = filled + held

    def start_of(position):
        def step(i, carry):
            running, best = carry
            best = jnp.where(running <= position, running, best)
            return running + lengths[i], best

        return lax.fori_loop(0, docs, step, (jnp.int32(0), jnp.int32(0)))[1]

    lowest = start_of(base)
    needed = before - lowest // BLOCK + 1

    def fetch(entry, which):
        place = table[entry]
        window, buffer, sem = ((kw, kbuf, 0), (vw, vbuf, 1))[which]
        source = window.at[
            place // SLOTS, pl.ds(pl.multiple_of(lax.rem(place, SLOTS) * BLOCK, BLOCK), BLOCK)
        ]
        return pltpu.make_async_copy(source, buffer.at[entry], sems.at[sem, entry])

    def start_fetch(which):
        def one(i, carry):
            fetch(1 + i, which).start()
            return carry

        lax.fori_loop(0, needed, one, 0)

        @pl.when(count == SLOTS)
        def _():
            fetch(0, which).start()

    start_fetch(0)
    start_fetch(1)

    scale = math.log2(math.e) / math.sqrt(128)
    ones = jnp.ones((BLOCK, 128), jnp.bfloat16)

    def block(slot):
        begin = base + slot * BLOCK
        low = lowest if slot == 0 else start_of(begin)
        high = start_of(begin + BLOCK - 1)
        number = (begin - low // BLOCK * BLOCK) // BLOCK + 1
        position = begin + lax.broadcasted_iota(jnp.int32, (BLOCK, 128), 0)
        first[...] = jnp.full((BLOCK, 128), low, jnp.int32)

        def mark(i, running):
            @pl.when((running > begin) & (running < begin + BLOCK))
            def _():
                first[...] = jnp.where(position >= running, running, first[...])

            return running + lengths[i]

        @pl.when(high != low)
        def _():
            lax.fori_loop(0, docs, mark, jnp.int32(0))

        top[...] = jnp.full(top.shape, NEGATIVE, jnp.float32)
        span = pl.ds(slot * BLOCK, BLOCK)

        def score(j, carry):
            entry = 1 - slot + j
            if slot == 0:
                fetch(entry, 0).wait()
            else:

                @pl.when(j == 0)
                def _():
                    fetch(0, 0).wait()

            key_begin = begin - j * BLOCK
            products = []
            for h in range(heads):
                products.append(
                    lax.dot_general(
                        q_ref[span, h * 128 : (h + 1) * 128],
                        kbuf[entry],
                        (((1,), (1,)), ((), ())),
                        preferred_element_type=jnp.float32,
                    )
                )

            def keep(mask):
                for h in range(heads):
                    best = top[h]
                    for part in range(BLOCK // 128):
                        lanes = slice(part * 128, (part + 1) * 128)
                        piece = products[h][:, lanes]
                        if mask is not None:
                            piece = jnp.where(mask[part], piece, NEGATIVE)
                        scores[j, h, :, lanes] = piece
                        best = jnp.maximum(best, piece)
                    top[h] = best

            plain = (j > 0) & (key_begin >= high)

            @pl.when(plain)
            def _():
                keep(None)

            @pl.when(jnp.logical_not(plain))
            def _():
                masks = []
                for part in range(BLOCK // 128):
                    key = key_begin + part * 128 + lax.broadcasted_iota(jnp.int32, (BLOCK, 128), 1)
                    masks.append((key >= first[...]) & (key <= position))
                keep(masks)

            return carry

        lax.fori_loop(0, number, score, 0)

        for h in range(heads):
            best = jnp.max(top[h], axis=1, keepdims=True) * scale
            top[h] = jnp.broadcast_to(best, (BLOCK, 128))
        total[...] = jnp.zeros(total.shape, jnp.float32)

        def weigh(j, carry):
            entry = 1 - slot + j
            if slot == 0:
                fetch(entry, 1).wait()
            else:

                @pl.when(j == 0)
                def _():
                    fetch(0, 1).wait()

            widened = jnp.concatenate([vbuf[entry], ones], axis=1)
            for h in range(heads):
                weights = []
                for part in range(BLOCK // 128):
                    lanes = slice(part * 128, (part + 1) * 128)
                    weights.append(jnp.exp2(scores[j, h, :, lanes] * scale - top[h]).astype(jnp.bfloat16))
                total[h] += jnp.dot(
                    jnp.concatenate(weights, axis=1), widened, preferred_element_type=jnp.float32
                )
            return carry

        lax.fori_loop(0, number, weigh, 0)
        for h in range(heads):
            result = total[h, :, :128] / total[h, :, 128:]
            out_ref[span, h * 128 : (h + 1) * 128] = result.astype(out_ref.dtype)

    block(0)

    @pl.when(count == SLOTS)
    def _():
        block(1)

    @pl.when(count != SLOTS)
    def _():
        out_ref[BLOCK:, :] = jnp.zeros((BLOCK, out_ref.shape[1]), out_ref.dtype)


def attend(lengths, counts, queries, kw, vw):
    heads = queries.shape[1] // 128
    entries = REACH + 2
    return pl.pallas_call(
        attend_kernel,
        out_shape=jax.ShapeDtypeStruct(queries.shape, jnp.bfloat16),
        in_specs=[
            pl.BlockSpec(memory_space=pltpu.SMEM),
            pl.BlockSpec(memory_space=pltpu.SMEM),
            pl.BlockSpec(memory_space=pltpu.VMEM),
            pl.BlockSpec(memory_space=pl.ANY),
            pl.BlockSpec(memory_space=pl.ANY),
        ],
        out_specs=pl.BlockSpec(memory_space=pltpu.VMEM),
        scratch_shapes=[
            pltpu.VMEM((entries, BLOCK, 128), jnp.bfloat16),
            pltpu.VMEM((entries, BLOCK, 128), jnp.bfloat16),
            pltpu.VMEM((REACH + 1, heads, BLOCK, BLOCK), jnp.float32),
            pltpu.VMEM((heads, BLOCK, 128), jnp.float32),
            pltpu.VMEM((heads, BLOCK, 256), jnp.float32),
            pltpu.VMEM((BLOCK, 128), jnp.int32),
            pltpu.SMEM((2 * REACH + 4,), jnp.int32),
            pltpu.SemaphoreType.DMA((2, entries)),
        ],
        compiler_params=pltpu.CompilerParams(vmem_limit_bytes=48 * 2**20),
        name="attend",
    )(lengths, counts, queries, kw, vw)


def shards(queries, keys, values, doc_lengths, block_count):
    kw, vw = gather_windows(keys, values)
    return attend(doc_lengths, block_count, queries, kw, vw)


def solution(mesh):
    placed = (
        P(("outer", "inner"), "head"),
        P(("outer", "inner", "head"), None),
        P(("outer", "inner", "head"), None),
        P(),
        P(),
    )
    return jax.shard_map(
        shards, mesh=mesh, in_specs=placed, out_specs=P(("outer", "inner"), "head"), check_vma=False
    )
```

time: 314 us -> 58.9 us (0.19)
  the two profiles are of different devices: /device:TPU:128 before, /device:TPU:40 now
where the time goes in v1:
time: 58.9 us; the launch traced here: 58.7 us
  Pallas kernels  53 us (90%)
  local copies, waits for them, and re-layouts  5.67 us (10%)
    pallas_call x1, Pallas kernels, gather_windows(): pl.pallas_call(gather_kernel, out_shape=(window, window), in_specs=[pl.Bl...  32.9 us
    pallas_call x1, Pallas kernels, attend(): pl.pallas_call(attend_kernel, out_shape=jax.ShapeDtypeStruct(queries.shap...  20.1 us
    unnamed x10, local copies, waits for them, and re-layouts  5.67 us

profile of v1, /device:TPU:40, one launch (start us, length us, event | category | flops | bytes accessed | tf_op | source)
XLA Modules:
  0.0 58.7 jit_solution(9111353648672571533)
XLA Ops:
  0.0 32.9 %gather_windows.1 = (bf16[9,1024,128]{2,1,0:T(8,128)(2,1)}, bf16[9,1024,128]{2,1,0:T(8,128)(2,1)}) custom-call(bf16[256,128]{1,0:T(8,128)(2,1)} %k_ref.1, bf16[256,128]{1,0:T(8,128)(2,1)} %v_ref.1), custom_call_target="tpu_custom_call" | custom-call | tf_op jit(solution)/shard_map/gather_windows/pallas_call | solution.py:283
  32.9 0.0 copy-start
  32.9 1.7 %copy-done = bf16[9,1024,128]{2,1,0:T(8,128)(2,1)S(1)} copy-done((bf16[9,1024,128]{2,1,0:T(8,128)(2,1)S(1)}, bf16[9,1024,128]{2,1,0:T(8,128)(2,1)}, u32[]{:S(2)}) %copy-start) | copy-done | bytes 2359320
  34.5 0.0 copy-start.1
  34.5 1.7 %copy-done.1 = bf16[9,1024,128]{2,1,0:T(8,128)(2,1)S(1)} copy-done((bf16[9,1024,128]{2,1,0:T(8,128)(2,1)S(1)}, bf16[9,1024,128]{2,1,0:T(8,128)(2,1)}, u32[]{:S(2)}) %copy-start.1) | copy-done | bytes 2359320
  36.2 0.0 copy-start.2
  36.2 1.0 %copy-done.2 = bf16[1024,256]{1,0:T(8,128)(2,1)S(1)} copy-done((bf16[1024,256]{1,0:T(8,128)(2,1)S(1)}, bf16[1024,256]{1,0:T(8,128)(2,1)}, u32[]{:S(2)}) %copy-start.2) | copy-done | bytes 524312
  37.2 0.0 copy-start.3
  37.2 0.7 %copy-done.3 = s32[28]{0:T(128)S(1)} copy-done((s32[28]{0:T(128)S(1)}, s32[28]{0:T(128)}, u32[]{:S(2)}) %copy-start.3) | copy-done | bytes 136
  37.9 0.0 copy-start.4
  37.9 0.7 %copy-done.4 = s32[64]{0:T(128)S(1)} copy-done((s32[64]{0:T(128)S(1)}, s32[64]{0:T(128)}, u32[]{:S(2)}) %copy-start.4) | copy-done | bytes 280
  38.5 20.1 %attend.1 = bf16[1024,256]{1,0:T(8,128)(2,1)} custom-call(s32[28]{0:T(128)S(1)} %copy-done.3, s32[64]{0:T(128)S(1)} %copy-done.4, bf16[1024,256]{1,0:T(8,128)(2,1)S(1)} %copy-done.2, bf16[9,1024,128]{2,1,0:T(8,128)(2,1)S(1)} %copy-done, bf16[9,1024,128]{2,1,0:T(8,128)(2,1)S(1)} %copy-done.1), custom_call_target="tpu_custom_call" | custom-call | tf_op jit(solution)/shard_map/attend/pallas_call | solution.py:474
Async XLA Ops:
  32.9 1.7 %copy-start = (bf16[9,1024,128]{2,1,0:T(8,128)(2,1)S(1)}, bf16[9,1024,128]{2,1,0:T(8,128)(2,1)}, u32[]{:S(2)}) copy-start(bf16[9,1024,128]{2,1,0:T(8,128)(2,1)} %get-tuple-element.7.kw) | copy-start | bytes 7077892
  34.5 1.7 %copy-start.1 = (bf16[9,1024,128]{2,1,0:T(8,128)(2,1)S(1)}, bf16[9,1024,128]{2,1,0:T(8,128)(2,1)}, u32[]{:S(2)}) copy-start(bf16[9,1024,128]{2,1,0:T(8,128)(2,1)} %get-tuple-element.8.vw) | copy-start | bytes 7077892
  36.2 1.0 %copy-start.2 = (bf16[1024,256]{1,0:T(8,128)(2,1)S(1)}, bf16[1024,256]{1,0:T(8,128)(2,1)}, u32[]{:S(2)}) copy-start(bf16[1024,256]{1,0:T(8,128)(2,1)} %q_ref.1) | copy-start | bytes 1572868
  37.2 0.7 %copy-start.3 = (s32[28]{0:T(128)S(1)}, s32[28]{0:T(128)}, u32[]{:S(2)}) copy-start(s32[28]{0:T(128)} %lengths.1) | copy-start | bytes 340
  37.9 0.7 %copy-start.4 = (s32[64]{0:T(128)S(1)}, s32[64]{0:T(128)}, u32[]{:S(2)}) copy-start(s32[64]{0:T(128)} %counts.1) | copy-start | bytes 772

commit v2 on v0

v2 whole, which is shorter than its diff:
```python
import math

import jax
import jax.numpy as jnp
from jax import lax
from jax.experimental import pallas as pl
from jax.experimental.pallas import tpu as pltpu
from jax.sharding import PartitionSpec as P

BLOCK = 512
SLOTS = 2
REACH = 7
QUARTER = 256
HALF = 128
MESH = pl.DeviceIdType.MESH
NEGATIVE = -1e30


def gather_kernel(k_ref, v_ref, kw, vw, send_sems, recv_sems, local_sems):
    outer = lax.axis_index("outer")
    inner = lax.axis_index("inner")
    y = lax.axis_index("head")
    z = outer * 2 + inner // 8
    x = lax.rem(inner // 2, 4)
    core = lax.rem(inner, 2)

    def place(px, py, pz, pc):
        return (pz // 2, lax.rem(pz, 2) * 8 + px * 2 + pc, py)

    xp, xm = lax.rem(x + 1, 4), lax.rem(x + 3, 4)
    yp, ym = lax.rem(y + 1, 4), lax.rem(y + 3, 4)
    zp, zm = lax.rem(z + 1, 8), lax.rem(z + 7, 8)
    z_next = jnp.where(x == 3, zp, z)
    z_prev = jnp.where(x == 0, zm, z)
    right, left = place(xp, y, z, core), place(xm, y, z, core)
    up, down = place(x, y, zp, core), place(x, y, zm, core)
    after, before = place(x, yp, z, core), place(x, ym, z, core)
    follower, leader = place(xp, y, z_next, core), place(xm, y, z_prev, core)
    sibling = place(x, y, z, 1 - core)

    barrier = pltpu.get_barrier_semaphore()
    for partner in (right, left, up, down, after, before, follower, leader, sibling):
        pl.semaphore_signal(barrier, inc=1, device_id=partner, device_id_type=MESH)

    def rows(order, half=None):
        start = lax.rem(y + order, 4) * QUARTER
        if half is None:
            return pl.ds(pl.multiple_of(start, QUARTER), QUARTER)
        return pl.ds(pl.multiple_of(start + half * HALF, HALF), HALF)

    sems, arrived, sent = {}, set(), []

    def transfer(name, src, dst, device):
        sem = sems.setdefault(name, len(sems))
        return pltpu.make_async_remote_copy(
            src_ref=src,
            dst_ref=dst,
            send_sem=send_sems.at[sem],
            recv_sem=recv_sems.at[sem],
            device_id=device,
            device_id_type=MESH,
        )

    shapes = {}

    def post(name, src, dst, device, when=None, track=True):
        copy = transfer(name, src, dst, device)
        if when is None:
            copy.start()
        else:
            pl.when(when)(copy.start)
        shapes[name] = dst
        if track:
            sent.append(name)

    def finish(name, dst):
        return transfer(name, dst, dst, sibling)

    def need(*names):
        for name in names:
            if name not in arrived:
                arrived.add(name)
                finish(name, places[name]).wait_recv()

    places = {}
    for order in range(4):
        part = rows(order)
        places["ku", order] = kw.at[8, part]
        places["kr", order] = kw.at[2, part]
        places["kl", order] = kw.at[6, part]
        places["km", order] = kw.at[4, part]
    for half in range(2):
        part = rows(0, half)
        places["vu", half] = vw.at[8, part]
        places["vr", half] = vw.at[2, part]
        places["vl", half] = vw.at[6, part]
        places["vm", half] = vw.at[4, part]
    for win, ring, slots in ((kw, "k", (0,)), (vw, "v", (0, 2, 4, 6, 8))):
        for slot in slots:
            places[ring, slot, 0] = win.at[slot, rows(3)]
            places[ring, slot, 1] = win.at[slot, rows(1)]
            places[ring, slot, 2] = win.at[slot, rows(2, 0)]
            places[ring, slot, 3] = win.at[slot, rows(2, 1)]

    keep_k = pltpu.make_async_copy(k_ref, kw.at[0, rows(0)], local_sems.at[0])
    keep_v = pltpu.make_async_copy(v_ref, vw.at[0, rows(0)], local_sems.at[1])
    keep_k.start()
    keep_v.start()
    pl.semaphore_wait(barrier, 9)

    def key_open():
        post(("k", 0, 0), k_ref, kw.at[0, rows(0)], after)
        post(("k", 0, 1), k_ref, kw.at[0, rows(0)], before)

    def key_pass(side):
        need(("k", 0, side))
        part = rows((3, 1)[side], side)
        post(("k", 0, 2 + side), kw.at[0, part], kw.at[0, part], (after, before)[side])

    def send(kind, win, index, part, own):
        post((kind + "u", index), own, win.at[8, part], up)
        post((kind + "r", index), own, win.at[2, part], right, x < 3)
        post((kind + "l", index), own, win.at[6, part], left, x == 0)

    def turn(kind, win, index, part):
        need((kind + "u", index))
        post((kind + "r", index), win.at[8, part], win.at[2, part], right, x == 3, False)
        post((kind + "l", index), win.at[8, part], win.at[6, part], left, x > 0, False)

    def relay(kind, win, index, part, forward):
        slot, source = (2, "r") if forward else (6, "l")
        need((kind + source, index))
        post((kind + "m", index), win.at[slot, part], win.at[4, part], follower if forward else leader)

    def key_send(order):
        if order == 3:
            need(("k", 0, 0))
        if order == 1:
            need(("k", 0, 1))
        if order == 2:
            need(("k", 0, 2), ("k", 0, 3))
        send("k", kw, order, rows(order), k_ref if order == 0 else kw.at[0, rows(order)])

    def key_turn(order):
        turn("k", kw, order, rows(order))

    def key_relay(order):
        relay("k", kw, order, rows(order), order in (0, 3))

    def value_send(half):
        send("v", vw, half, rows(0, half), v_ref.at[pl.ds(half * HALF, HALF)])

    def value_turn(half):
        turn("v", vw, half, rows(0, half))

    def value_relay(half):
        relay("v", vw, half, rows(0, half), half == 0)

    def only(slot, run):
        if slot == 8:
            pl.when(core == 1)(run)
        else:
            run()

    def ring_open(slot):
        if slot:
            source = {2: "vr", 4: "vm", 6: "vl", 8: "vu"}[slot]
            need((source, 0), (source, 1))
        own = vw.at[slot, rows(0)]

        def run():
            post(("v", slot, 0), own if slot else v_ref, own, after, track=slot != 8)
            post(("v", slot, 1), own if slot else v_ref, own, before, track=slot != 8)

        only(slot, run)

    def ring_pass(slot):
        parts = [vw.at[slot, rows(3, 0)], vw.at[slot, rows(1, 1)]]

        def run():
            for side, part in enumerate(parts):
                need(("v", slot, side))
                post(
                    ("v", slot, 2 + side),
                    part,
                    part,
                    (after, before)[side],
                    track=slot != 8,
                )

        only(slot, run)

    kept = []

    def keep():
        if not kept:
            kept.append(True)
            keep_k.wait()
            keep_v.wait()

    def share(win, slot):
        kind = "k" if win is kw else "v"
        if slot == 0:
            keep()
        if kind == "k" and slot:
            source = {2: "kr", 6: "kl", 8: "ku"}[slot]
            need(*((source, order) for order in range(4)))
        elif kind == "k":
            need(*(("k", 0, i) for i in range(4)))

        there = win.at[slot + 1 - 2 * core]

        def run():
            if kind == "v":
                need(*(("v", slot, i) for i in range(4)))
            if slot == 0:
                post((kind + "c", slot), win.at[slot], there, sibling, core == 0, False)
            else:
                post((kind + "c", slot), win.at[slot], there, sibling, track=slot != 8)

        only(slot, run)

    def share_middle_keys(order):
        need(("km", order))
        part = rows(order)
        post(("kc", 4, order), kw.at[4, part], kw.at[5 - 2 * core, part], sibling)

    def share_middle_values(step):
        if step == 0:
            need(("vm", 0), ("vm", 1), ("v", 4, 0), ("v", 4, 1))
            parts = (0, 3, 1)
        else:
            need(("v", 4, 2), ("v", 4, 3))
            parts = (2,)
        for order in parts:
            part = rows(order)
            post(("vc", 4, order), vw.at[4, part], vw.at[5 - 2 * core, part], sibling)

    value_send(0)
    value_send(1)
    key_open()
    key_send(0)
    key_send(1)
    ring_open(0)
    value_turn(0)
    key_send(3)
    ring_open(8)
    value_turn(1)
    key_turn(0)
    key_pass(1)
    value_relay(0)
    key_pass(0)
    value_relay(1)
    ring_pass(0)
    key_turn(1)
    ring_pass(8)
    ring_open(2)
    key_send(2)
    ring_open(6)
    key_turn(3)
    key_turn(2)
    key_relay(0)
    share(vw, 0)
    ring_open(4)
    share(kw, 8)
    key_relay(1)
    share(vw, 8)
    ring_pass(6)
    key_relay(3)
    share(kw, 6)
    ring_pass(2)
    key_relay(2)
    ring_pass(4)
    share(kw, 0)
    share_middle_keys(1)
    share(kw, 2)
    share(vw, 6)
    share_middle_values(0)
    share_middle_keys(0)
    share(vw, 2)
    share_middle_keys(3)
    share_middle_values(1)
    share_middle_keys(2)
    keep()
    for kind, win in (("k", kw), ("v", vw)):
        for order in range(4):
            finish((kind + "c", 4, order), win.at[5, rows(order)]).wait_recv()
        for slot in (2, 6):
            finish((kind + "c", slot), win.at[slot]).wait_recv()

        @pl.when(core == 1)
        def _(kind=kind, win=win):
            finish((kind + "c", 0), win.at[0]).wait_recv()
            finish((kind + "c", 8), win.at[8]).wait_send()

        @pl.when(core == 0)
        def _(kind=kind, win=win):
            finish((kind + "c", 0), win.at[0]).wait_send()
            finish((kind + "c", 8), win.at[8]).wait_recv()

    @pl.when(core == 1)
    def _():
        for i in range(4):
            finish(("v", 8, i), shapes["v", 8, i]).wait_send()

    for name in sent:
        finish(name, shapes[name]).wait_send()


def gather_windows(keys, values):
    depth = keys.shape[1]
    window = jax.ShapeDtypeStruct((REACH + 2, BLOCK * SLOTS, depth), keys.dtype)
    count = 96
    return pl.pallas_call(
        gather_kernel,
        out_shape=(window, window),
        in_specs=[pl.BlockSpec(memory_space=pl.ANY)] * 2,
        out_specs=(pl.BlockSpec(memory_space=pl.ANY),) * 2,
        scratch_shapes=[
            pltpu.SemaphoreType.DMA((count,)),
            pltpu.SemaphoreType.DMA((count,)),
            pltpu.SemaphoreType.DMA((2,)),
        ],
        compiler_params=pltpu.CompilerParams(collective_id=0, has_side_effects=True),
        name="gather_windows",
    )(keys, values)


def attend_kernel(
    lengths, counts, q_hbm, kw, vw, out_hbm, qbuf, kbuf, vbuf, scores, top, total, first, obuf, table, sems, io_sems
):
    heads = q_hbm.shape[1] // 128
    contexts = counts.shape[0]
    docs = lengths.shape[0]
    spans = [pl.ds(slot * BLOCK, BLOCK) for slot in range(SLOTS)]
    q_in = [
        pltpu.make_async_copy(
            q_hbm.at[spans[slot], h * 128 : (h + 1) * 128],
            qbuf.at[slot, pl.ds(h * BLOCK, BLOCK)],
            io_sems.at[0, slot * heads + h],
        )
        for slot in range(SLOTS)
        for h in range(heads)
    ]
    outs = [pltpu.make_async_copy(obuf.at[s], out_hbm.at[s], io_sems.at[1, i]) for i, s in enumerate(spans)]
    for copy in q_in:
        copy.start()

    me = lax.axis_index("outer") * 16 + lax.axis_index("inner")
    count = counts[me]
    before = jnp.int32(0)
    for i in range(contexts):
        before = before + jnp.where(i < me, counts[i], 0)
    base = before * BLOCK
    ends = []
    running = jnp.int32(0)
    for i in range(docs):
        running = running + lengths[i]
        ends.append(running)

    def start_of(position):
        best = jnp.int32(0)
        for end in ends:
            best = jnp.where(end <= position, end, best)
        return best

    table[0] = 1
    table[1] = 0
    filled = jnp.int32(2)
    for distance in range(1, REACH + 1):
        source = me - distance
        held = jnp.where(source >= 0, counts[jnp.maximum(source, 0)], 0)
        table[filled] = distance * SLOTS + held - 1
        table[filled + 1] = distance * SLOTS
        filled = filled + held

    lowest = start_of(base)
    needed = before - lowest // BLOCK + 1

    def fetch(entry, which):
        place = table[entry]
        window, buffer, sem = ((kw, kbuf, 0), (vw, vbuf, 1))[which]
        source = window.at[
            place // SLOTS, pl.ds(pl.multiple_of(lax.rem(place, SLOTS) * BLOCK, BLOCK), BLOCK)
        ]
        return pltpu.make_async_copy(source, buffer.at[entry], sems.at[sem, entry])

    for which in range(2):

        def one(i, carry):
            fetch(1 + i, which).start()
            return carry

        lax.fori_loop(0, needed, one, 0)

        @pl.when(count == SLOTS)
        def _():
            fetch(0, which).start()

    scale = math.log2(math.e) / math.sqrt(128)

    def block(slot):
        begin = base + slot * BLOCK
        low = lowest if slot == 0 else start_of(begin)
        high = start_of(begin + BLOCK - 1)
        number = (begin - low // BLOCK * BLOCK) // BLOCK + 1
        plain_end = jnp.maximum((begin - high) // BLOCK, 0) + 1
        position = begin + lax.broadcasted_iota(jnp.int32, (BLOCK, 128), 0)
        first[...] = jnp.full((BLOCK, 128), low, jnp.int32)

        def mark(i, running):
            @pl.when((running > begin) & (running < begin + BLOCK))
            def _():
                first[...] = jnp.where(position >= running, running, first[...])

            return running + lengths[i]

        @pl.when(high != low)
        def _():
            lax.fori_loop(0, docs, mark, jnp.int32(0))

        for h in range(heads):
            q_in[slot * heads + h].wait()

        def wait_for(j, width, which):
            if slot == 0:
                for step in range(width):
                    fetch(1 + j + step, which).wait()
            elif isinstance(j, int) and j == 0:
                fetch(0, which).wait()

        def score(j, width, masked, fresh):
            entry = 1 - slot + j
            wait_for(j, width, 0)
            product = lax.dot_general(
                qbuf[slot],
                kbuf[pl.ds(entry, width)].reshape(width * BLOCK, 128),
                (((1,), (1,)), ((), ())),
                preferred_element_type=jnp.float32,
            )
            best = [None if fresh else top[h] for h in range(heads)]
            for step in range(width):
                for part in range(BLOCK // 128):
                    if masked:
                        key = (
                            begin
                            - (j + step) * BLOCK
                            + part * 128
                            + lax.broadcasted_iota(jnp.int32, (BLOCK, 128), 1)
                        )
                        mask = (key >= first[...]) & (key <= position)
                    for h in range(heads):
                        rows = slice(h * BLOCK, (h + 1) * BLOCK)
                        piece = product[rows, step * BLOCK + part * 128 : step * BLOCK + (part + 1) * 128]
                        if masked:
                            piece = jnp.where(mask, piece, NEGATIVE)
                        scores[j + step, rows, part * 128 : (part + 1) * 128] = piece
                        best[h] = piece if best[h] is None else jnp.maximum(best[h], piece)
            for h in range(heads):
                top[h] = best[h]

        def weigh(j, width, fresh):
            entry = 1 - slot + j
            wait_for(j, width, 1)
            value = vbuf[pl.ds(entry, width)].reshape(width * BLOCK, 128)
            widened = jnp.concatenate([value, jnp.ones_like(value)], axis=1)
            highest = top[...].reshape(heads * BLOCK, 128)
            weights = []
            for step in range(width):
                for part in range(BLOCK // 128):
                    shifted = scores[j + step, :, part * 128 : (part + 1) * 128] * scale - highest
                    weights.append(jnp.exp2(shifted).astype(jnp.bfloat16))
            product = jnp.dot(
                jnp.concatenate(weights, axis=1), widened, preferred_element_type=jnp.float32
            )
            if fresh:
                total[...] = product
            else:
                total[...] += product

        pairs = number // 2
        plain_pairs = jnp.clip(plain_end // 2, 1, jnp.maximum(pairs, 1))
        alone = number == 1
        odd = (number > 1) & (lax.rem(number, 2) == 1)

        def looped(body):
            def step(i, carry):
                body(2 * i)
                return carry

            return step

        @pl.when(alone)
        def _():
            score(0, 1, True, True)

        @pl.when(jnp.logical_not(alone))
        def _():
            score(0, 2, True, True)

        lax.fori_loop(1, plain_pairs, looped(lambda j: score(j, 2, False, False)), 0)
        lax.fori_loop(plain_pairs, pairs, looped(lambda j: score(j, 2, True, False)), 0)

        @pl.when(odd)
        def _():
            score(number - 1, 1, True, False)

        for h in range(heads):
            best = jnp.max(top[h], axis=1, keepdims=True) * scale
            top[h] = jnp.broadcast_to(best, (BLOCK, 128))

        @pl.when(alone)
        def _():
            weigh(0, 1, True)

        @pl.when(jnp.logical_not(alone))
        def _():
            weigh(0, 2, True)

        lax.fori_loop(1, pairs, looped(lambda j: weigh(j, 2, False)), 0)

        @pl.when(odd)
        def _():
            weigh(number - 1, 1, False)

        for h in range(heads):
            rows = slice(h * BLOCK, (h + 1) * BLOCK)
            result = total[rows, :128] / total[rows, 128:]
            obuf[spans[slot], h * 128 : (h + 1) * 128] = result.astype(obuf.dtype)
        outs[slot].start()

    block(0)

    @pl.when(count == SLOTS)
    def _():
        block(1)

    @pl.when(count != SLOTS)
    def _():
        obuf[spans[1], :] = jnp.zeros((BLOCK, obuf.shape[1]), obuf.dtype)
        for h in range(heads):
            q_in[heads + h].wait()
        outs[1].start()

    for copy in outs:
        copy.wait()


def attend(lengths, counts, queries, kw, vw):
    heads = queries.shape[1] // 128
    entries = REACH + 2
    return pl.pallas_call(
        attend_kernel,
        out_shape=jax.ShapeDtypeStruct(queries.shape, jnp.bfloat16),
        in_specs=[
            pl.BlockSpec(memory_space=pltpu.SMEM),
            pl.BlockSpec(memory_space=pltpu.SMEM),
            pl.BlockSpec(memory_space=pl.ANY),
            pl.BlockSpec(memory_space=pl.ANY),
            pl.BlockSpec(memory_space=pl.ANY),
        ],
        out_specs=pl.BlockSpec(memory_space=pl.ANY),
        scratch_shapes=[
            pltpu.VMEM((SLOTS, heads * BLOCK, 128), jnp.bfloat16),
            pltpu.VMEM((entries, BLOCK, 128), jnp.bfloat16),
            pltpu.VMEM((entries, BLOCK, 128), jnp.bfloat16),
            pltpu.VMEM((REACH + 1, heads * BLOCK, BLOCK), jnp.float32),
            pltpu.VMEM((heads, BLOCK, 128), jnp.float32),
            pltpu.VMEM((heads * BLOCK, 256), jnp.float32),
            pltpu.VMEM((BLOCK, 128), jnp.int32),
            pltpu.VMEM(queries.shape, jnp.bfloat16),
            pltpu.SMEM((2 * REACH + 4,), jnp.int32),
            pltpu.SemaphoreType.DMA((2, entries)),
            pltpu.SemaphoreType.DMA((2, SLOTS * heads)),
        ],
        compiler_params=pltpu.CompilerParams(vmem_limit_bytes=60 * 2**20),
        name="attend",
    )(lengths, counts, queries, kw, vw)


def shards(queries, keys, values, doc_lengths, block_count):
    kw, vw = gather_windows(keys, values)
    return attend(doc_lengths, block_count, queries, kw, vw)


def solution(mesh):
    placed = (
        P(("outer", "inner"), "head"),
        P(("outer", "inner", "head"), None),
        P(("outer", "inner", "head"), None),
        P(),
        P(),
    )
    return jax.shard_map(
        shards, mesh=mesh, in_specs=placed, out_specs=P(("outer", "inner"), "head"), check_vma=False
    )
```

time: 314 us -> 45.8 us (0.15)
  the two profiles are of different devices: /device:TPU:128 before, /device:TPU:1 now
where the time goes in v2:
time: 45.8 us; the launch traced here: 45.7 us
  Pallas kernels  45.7 us (100%)
    pallas_call x1, Pallas kernels, gather_windows(): pl.pallas_call(gather_kernel, out_shape=(window, window), in_specs=[pl.Bl...  36 us
    pallas_call x1, Pallas kernels, attend(): pl.pallas_call(attend_kernel, out_shape=jax.ShapeDtypeStruct(queries.shap...  9.77 us

profile of v2, /device:TPU:1, one launch (start us, length us, event | category | flops | bytes accessed | tf_op | source)
XLA Modules:
  0.0 45.7 jit_solution(12014823554054887279)
XLA Ops:
  0.0 36.0 %gather_windows.1 = (bf16[9,1024,128]{2,1,0:T(8,128)(2,1)}, bf16[9,1024,128]{2,1,0:T(8,128)(2,1)}) custom-call(bf16[256,128]{1,0:T(8,128)(2,1)} %k_ref.1, bf16[256,128]{1,0:T(8,128)(2,1)} %v_ref.1), custom_call_target="tpu_custom_call" | custom-call | tf_op jit(solution)/shard_map/gather_windows/pallas_call | solution.py:314
  36.0 9.8 %attend.1 = bf16[1024,256]{1,0:T(8,128)(2,1)} custom-call(s32[28]{0:T(128)} %lengths.1, s32[64]{0:T(128)} %counts.1, bf16[1024,256]{1,0:T(8,128)(2,1)} %q_hbm.1, bf16[9,1024,128]{2,1,0:T(8,128)(2,1)} %get-tuple-element.7.kw, bf16[9,1024,128]{2,1,0:T(8,128)(2,1)} %get-tuple-element.8.vw), custom_call_target="tpu_custom_call" | custom-call | tf_op jit(solution)/shard_map/attend/pallas_call | solution.py:552

commit v3 on v2

--- a/solution.py
+++ b/solution.py
@@ -11,6 +11,7 @@
 SLOTS = 2
 REACH = 7
 QUARTER = 256
+LAYERS = 8
 HALF = 128
 MESH = pl.DeviceIdType.MESH
 NEGATIVE = -1e30
@@ -29,7 +30,7 @@
 
     xp, xm = lax.rem(x + 1, 4), lax.rem(x + 3, 4)
     yp, ym = lax.rem(y + 1, 4), lax.rem(y + 3, 4)
-    zp, zm = lax.rem(z + 1, 8), lax.rem(z + 7, 8)
+    zp, zm = lax.rem(z + 1, LAYERS), lax.rem(z + LAYERS - 1, LAYERS)
     z_next = jnp.where(x == 3, zp, z)
     z_prev = jnp.where(x == 0, zm, z)
     right, left = place(xp, y, z, core), place(xm, y, z, core)
@@ -38,9 +39,36 @@
     follower, leader = place(xp, y, z_next, core), place(xm, y, z_prev, core)
     sibling = place(x, y, z, 1 - core)
 
+    chip = z * 4 + x
+    last = LAYERS * 4 - 1
+    has_up, has_down = z < LAYERS - 1, z > 0
     barrier = pltpu.get_barrier_semaphore()
-    for partner in (right, left, up, down, after, before, follower, leader, sibling):
+
+    def greet(partner):
         pl.semaphore_signal(barrier, inc=1, device_id=partner, device_id_type=MESH)
+
+    for partner in (right, left, after, before, sibling):
+        greet(partner)
+    pl.when(has_up)(lambda: greet(up))
+    pl.when(has_down)(lambda: greet(down))
+    pl.when(chip < last)(lambda: greet(follower))
+    pl.when(chip > 0)(lambda: greet(leader))
+
+    def one(flag):
+        return jnp.where(flag, 1, 0)
+
+    partners = 5 + one(has_up) + one(has_down) + one(chip < last) + one(chip > 0)
+
+    def present(name):
+        if name[0] in ("k", "v"):
+            return None if name[1] == 0 else chip >= name[1] // 2
+        return chip >= {"u": 4, "r": 1, "l": 3, "m": 2}[name[0][1]]
+
+    def under(flag, run):
+        if flag is None:
+            run()
+        else:
+            pl.when(flag)(run)
 
     def rows(order, half=None):
         start = lax.rem(y + order, 4) * QUARTER
@@ -50,28 +78,25 @@
 
     sems, arrived, sent = {}, set(), []
 
-    def transfer(name, src, dst, device):
+    def transfer(name, src, dst, device, arrives=None):
         sem = sems.setdefault(name, len(sems))
+        end = sems.setdefault(arrives or name, len(sems))
         return pltpu.make_async_remote_copy(
             src_ref=src,
             dst_ref=dst,
             send_sem=send_sems.at[sem],
-            recv_sem=recv_sems.at[sem],
+            recv_sem=recv_sems.at[end],
             device_id=device,
             device_id_type=MESH,
         )
 
     shapes = {}
 
-    def post(name, src, dst, device, when=None, track=True):
-        copy = transfer(name, src, dst, device)
-        if when is None:
-            copy.start()
-        else:
-            pl.when(when)(copy.start)
+    def post(name, src, dst, device, when=None, done=None, arrives=None, track=True):
+        under(when, transfer(name, src, dst, device, arrives).start)
         shapes[name] = dst
         if track:
-            sent.append(name)
+            sent.append((name, when if done is None else done))
 
     def finish(name, dst):
         return transfer(name, dst, dst, sibling)
@@ -80,7 +105,7 @@
         for name in names:
             if name not in arrived:
                 arrived.add(name)
-                finish(name, places[name]).wait_recv()
+                under(present(name), finish(name, places[name]).wait_recv)
 
     places = {}
     for order in range(4):
@@ -106,7 +131,7 @@
     keep_v = pltpu.make_async_copy(v_ref, vw.at[0, rows(0)], local_sems.at[1])
     keep_k.start()
     keep_v.start()
-    pl.semaphore_wait(barrier, 9)
+    pl.semaphore_wait(barrier, partners)
 
     def key_open():
         post(("k", 0, 0), k_ref, kw.at[0, rows(0)], after)
@@ -118,19 +143,25 @@
         post(("k", 0, 2 + side), kw.at[0, part], kw.at[0, part], (after, before)[side])
 
     def send(kind, win, index, part, own):
-        post((kind + "u", index), own, win.at[8, part], up)
-        post((kind + "r", index), own, win.at[2, part], right, x < 3)
-        post((kind + "l", index), own, win.at[6, part], left, x == 0)
+        post((kind + "u", index), own, win.at[8, part], up, has_up)
+        post((kind + "r", index), own, win.at[2, part], right, x < 3, (x < 3) | has_down)
+        post((kind + "l", index), own, win.at[6, part], left, x == 0, (x == 0) | has_down)
 
     def turn(kind, win, index, part):
         need((kind + "u", index))
-        post((kind + "r", index), win.at[8, part], win.at[2, part], right, x == 3, False)
-        post((kind + "l", index), win.at[8, part], win.at[6, part], left, x > 0, False)
+        post((kind + "r", index), win.at[8, part], win.at[2, part], right, (x == 3) & has_down, track=False)
+        post((kind + "l", index), win.at[8, part], win.at[6, part], left, (x > 0) & has_down, track=False)
 
     def relay(kind, win, index, part, forward):
-        slot, source = (2, "r") if forward else (6, "l")
-        need((kind + source, index))
-        post((kind + "m", index), win.at[slot, part], win.at[4, part], follower if forward else leader)
+        name, there = (kind + "m", index), win.at[4, part]
+        if forward:
+            need((kind + "r", index))
+            post(name, win.at[2, part], there, follower, (chip > 0) & (chip < last))
+        else:
+            need((kind + "l", index))
+            post(name, win.at[6, part], there, leader, chip >= 3)
+            need((kind + "r", index))
+            post((kind + "x", index), win.at[2, part], there, follower, chip == last - 1, arrives=name)
 
     def key_send(order):
         if order == 3:
@@ -158,9 +189,13 @@
 
     def only(slot, run):
         if slot == 8:
-            pl.when(core == 1)(run)
+            pl.when((core == 1) & (chip >= 4))(run)
+        elif slot:
+            pl.when(chip >= slot // 2)(run)
         else:
             run()
+
+    rings = []
 
     def ring_open(slot):
         if slot:
@@ -169,10 +204,11 @@
         own = vw.at[slot, rows(0)]
 
         def run():
-            post(("v", slot, 0), own if slot else v_ref, own, after, track=slot != 8)
-            post(("v", slot, 1), own if slot else v_ref, own, before, track=slot != 8)
+            post(("v", slot, 0), own if slot else v_ref, own, after, track=False)
+            post(("v", slot, 1), own if slot else v_ref, own, before, track=False)
 
         only(slot, run)
+        rings.append(slot)
 
     def ring_pass(slot):
         parts = [vw.at[slot, rows(3, 0)], vw.at[slot, rows(1, 1)]]
@@ -185,7 +221,7 @@
                     part,
                     part,
                     (after, before)[side],
-                    track=slot != 8,
+                    track=False,
                 )
 
         only(slot, run)
@@ -209,16 +245,15 @@
             need(*(("k", 0, i) for i in range(4)))
 
         there = win.at[slot + 1 - 2 * core]
-
-        def run():
-            if kind == "v":
-                need(*(("v", slot, i) for i in range(4)))
-            if slot == 0:
-                post((kind + "c", slot), win.at[slot], there, sibling, core == 0, False)
-            else:
-                post((kind + "c", slot), win.at[slot], there, sibling, track=slot != 8)
-
-        only(slot, run)
+        if kind == "v":
+            only(slot, lambda: need(*(("v", slot, i) for i in range(4))))
+        name = (kind + "c", slot)
+        if slot == 0:
+            post(name, win.at[slot], there, sibling, core == 0)
+        elif slot == 8:
+            post(name, win.at[slot], there, sibling, core == 1)
+        else:
+            post(name, win.at[slot], there, sibling)
 
     def share_middle_keys(order):
         need(("km", order))
@@ -287,30 +322,24 @@
             finish((kind + "c", 4, order), win.at[5, rows(order)]).wait_recv()
         for slot in (2, 6):
             finish((kind + "c", slot), win.at[slot]).wait_recv()
-
-        @pl.when(core == 1)
-        def _(kind=kind, win=win):
-            finish((kind + "c", 0), win.at[0]).wait_recv()
-            finish((kind + "c", 8), win.at[8]).wait_send()
-
-        @pl.when(core == 0)
-        def _(kind=kind, win=win):
-            finish((kind + "c", 0), win.at[0]).wait_send()
-            finish((kind + "c", 8), win.at[8]).wait_recv()
-
-    @pl.when(core == 1)
-    def _():
-        for i in range(4):
-            finish(("v", 8, i), shapes["v", 8, i]).wait_send()
-
-    for name in sent:
-        finish(name, shapes[name]).wait_send()
+        pl.when(core == 1)(finish((kind + "c", 0), win.at[0]).wait_recv)
+        pl.when(core == 0)(finish((kind + "c", 8), win.at[8]).wait_recv)
+
+    for name, when in sent:
+        under(when, finish(name, shapes[name]).wait_send)
+    for slot in rings:
+
+        def close(slot=slot):
+            for i in range(4):
+                finish(("v", slot, i), shapes["v", slot, i]).wait_send()
+
+        only(slot, close)
 
 
 def gather_windows(keys, values):
     depth = keys.shape[1]
     window = jax.ShapeDtypeStruct((REACH + 2, BLOCK * SLOTS, depth), keys.dtype)
-    count = 96
+    count = 112
     return pl.pallas_call(
         gather_kernel,
         out_shape=(window, window),

time: 45.8 us -> 41.5 us (0.906)
  the two profiles are of different devices: /device:TPU:1 before, /device:TPU:160 now
where the time goes in v3:
time: 41.5 us; the launch traced here: 41.4 us
  Pallas kernels  41.3 us (100%)
    pallas_call x1, Pallas kernels, gather_windows(): pl.pallas_call(gather_kernel, out_shape=(window, window), in_specs=[pl.Bl...  30 us
    pallas_call x1, Pallas kernels, attend(): pl.pallas_call(attend_kernel, out_shape=jax.ShapeDtypeStruct(queries.shap...  11.4 us

profile of v3, /device:TPU:160, one launch (start us, length us, event | category | flops | bytes accessed | tf_op | source)
XLA Modules:
  0.0 41.4 jit_solution(3189651464699432310)
XLA Ops:
  0.0 30.0 %gather_windows.1 = (bf16[9,1024,128]{2,1,0:T(8,128)(2,1)}, bf16[9,1024,128]{2,1,0:T(8,128)(2,1)}) custom-call(bf16[256,128]{1,0:T(8,128)(2,1)} %k_ref.1, bf16[256,128]{1,0:T(8,128)(2,1)} %v_ref.1), custom_call_target="tpu_custom_call" | custom-call | tf_op jit(solution)/shard_map/gather_windows/pallas_call | solution.py:343
  30.0 11.4 %attend.1 = bf16[1024,256]{1,0:T(8,128)(2,1)} custom-call(s32[28]{0:T(128)} %lengths.1, s32[64]{0:T(128)} %counts.1, bf16[1024,256]{1,0:T(8,128)(2,1)} %q_hbm.1, bf16[9,1024,128]{2,1,0:T(8,128)(2,1)} %get-tuple-element.7.kw, bf16[9,1024,128]{2,1,0:T(8,128)(2,1)} %get-tuple-element.8.vw), custom_call_target="tpu_custom_call" | custom-call | tf_op jit(solution)/shard_map/attend/pallas_call | solution.py:581
